TPU v7x, 512 devices: a whole 4x8x8 slice. The times are simulated.
512 devices in a mesh: row: 32 (over y, x), col: 16 (over z, core).
Axes of the slice: x: 4, y: 8, z: 8, core: 2. Of those that a mesh axis runs over, the one named last changes fastest.
Arguments:
- diag_tiles: float32 [32, 256, 256], P('row'), as said below
- left_fac: bfloat16 [32, 32, 256, 128], P('row', 'col'), as said below
- right_fac: bfloat16 [32, 32, 256, 128], P('row', 'col'), as said below
- ranks: int32 [32, 32], replicated, may hold values from 16 to 128, as said below
Outputs:
- factored: float32 [32, 32, 256, 256], P('row', 'col')
Inputs may be any that keep to these rules, and one draw needn't show every extreme that they name: `ranks`: every entry is a multiple of 16; in every draw some tile below the diagonal has rank 128, and the mean rank is about a third of 128. `diag_tiles`: every tile is symmetric; the first diagonal tile and the updated second diagonal tile M are positive definite. `left_fac`: entries have mean zero and deviation one. `right_fac`: entries have mean zero and deviation one over the square root of 128.
All inputs are finite; a program needn't handle non-finite values.
Results may differ from a plain program's by a relative error of at most 0.0003.
Values sent between devices are 32-bit elements; how exact they have to be, the bound alone decides.
A program may use at most 64 MiB of HBM per device.

v0:
```python
import jax
import jax.numpy as jnp
from jax import lax
from jax.sharding import PartitionSpec as P

PRECISE = lax.Precision.HIGHEST


def from_root(shard, axis, root):
    mine = lax.axis_index(axis) == root
    return lax.psum(jnp.where(mine, shard, jnp.zeros_like(shard)), axis)


def lower_solve(factor, stacked):
    pieces, tile_width, rank_cap = stacked.shape
    flattened = jnp.transpose(stacked, (1, 0, 2)).reshape(tile_width, pieces * rank_cap)
    solved = lax.linalg.triangular_solve(factor, flattened, left_side=True, lower=True)
    return jnp.transpose(solved.reshape(tile_width, pieces, rank_cap), (1, 0, 2))


def expand(left_basis, weights):
    return jnp.einsum("nbr,ncr->nbc", left_basis, weights, precision=PRECISE)


def correction(head_basis, row_solved, pivot_solved):
    mixing = jnp.einsum("nbr,bs->nrs", row_solved, pivot_solved, precision=PRECISE)
    return -jnp.einsum("bs,nrs->nbr", head_basis, mixing, precision=PRECISE)


def take_slot(stacked, holder_slot):
    return lax.dynamic_index_in_dim(stacked, holder_slot, 0, keepdims=False)


def shards(diag_tiles, left_fac, right_fac, ranks):
    grid_rows = lax.axis_size("row")
    grid_cols = lax.axis_size("col")
    row_here = lax.axis_index("row")
    col_here = lax.axis_index("col")
    row_slots, col_slots, tile_width, rank_cap = left_fac.shape
    tile_rows = jnp.arange(row_slots, dtype=jnp.int32) * grid_rows + row_here
    tile_cols = jnp.arange(col_slots, dtype=jnp.int32) * grid_cols + col_here
    local_ranks = jnp.take(jnp.take(ranks, tile_rows, axis=0), tile_cols, axis=1)
    columns_live = jnp.arange(rank_cap, dtype=jnp.int32)[None, None, :] < local_ranks[:, :, None]
    left_bases = jnp.where(columns_live[:, :, None, :], left_fac.astype(jnp.float32), 0.0)
    right_coefs = right_fac.astype(jnp.float32)
    first_pivot = from_root(jnp.linalg.cholesky(diag_tiles[0]), "row", 0)
    first_local = lower_solve(first_pivot, right_coefs[:, 0])
    first_row_basis, first_row_solved = (
        from_root(left_bases[:, 0], "col", 0),
        from_root(first_local, "col", 0),
    )
    gathered_basis = []
    gathered_solved = []
    for column_slot in range(col_slots):
        tile_number = column_slot * grid_cols + col_here
        holder_slot = tile_number // grid_rows
        received = (
            from_root(take_slot(first_row_basis, holder_slot), "row", tile_number % grid_rows),
            from_root(take_slot(first_row_solved, holder_slot), "row", tile_number % grid_rows),
        )
        gathered_basis.append(received[0])
        gathered_solved.append(received[1])
    first_col_basis = jnp.stack(gathered_basis)
    first_col_solved = jnp.stack(gathered_solved)
    pivot_basis = first_row_basis[0]
    pivot_solved = first_row_solved[0]
    pivot_cross = jnp.einsum("br,bs->rs", pivot_solved, pivot_solved, precision=PRECISE)
    partial_term = jnp.matmul(pivot_basis, pivot_cross, precision=PRECISE)
    shifted = diag_tiles[0] - jnp.matmul(partial_term, pivot_basis.T, precision=PRECISE)
    second_pivot = from_root(jnp.linalg.cholesky(shifted), "row", 1)
    second_local = lower_solve(second_pivot, right_coefs[:, 0])
    first_row_dense = expand(first_row_basis, first_row_solved)
    first_col_dense = expand(first_col_basis, first_col_solved)
    pieces_dense = []
    local_head = lax.linalg.triangular_solve(
        second_pivot, first_col_basis[0], left_side=True, lower=True
    )
    local_minus = correction(local_head, first_row_solved, first_col_solved[0])
    second_row = (
        from_root(left_bases[:, 0], "col", 1),
        from_root(second_local, "col", 1),
        from_root(local_minus, "col", 1),
    )
    second_row_dense = expand(second_row[0], second_row[1]) + expand(first_row_basis, second_row[2])
    for column_slot in range(col_slots):
        tile_number = column_slot * grid_cols + col_here
        holder_slot = tile_number // grid_rows
        received = (
            from_root(take_slot(second_row[0], holder_slot), "row", tile_number % grid_rows),
            from_root(take_slot(second_row[1], holder_slot), "row", tile_number % grid_rows),
            from_root(take_slot(second_row[2], holder_slot), "row", tile_number % grid_rows),
        )
        own_dense = expand(received[0][None], received[1][None]) + expand(
            first_col_basis[column_slot][None], received[2][None]
        )
        pieces_dense.append(own_dense[0])
    second_col_dense = jnp.stack(pieces_dense)
    dense_front = jnp.einsum("lmbr,lmcr->lmbc", left_bases, right_coefs, precision=PRECISE)
    updates = jnp.einsum("lbk,mck->lmbc", first_row_dense, first_col_dense, precision=PRECISE)
    updates = updates + jnp.einsum(
        "lbk,mck->lmbc", second_row_dense, second_col_dense, precision=PRECISE
    )
    schur = dense_front - updates
    row_ids = tile_rows[:, None, None, None]
    col_ids = tile_cols[None, :, None, None]
    chosen = jnp.where(
        col_ids == 0,
        first_row_dense[:, None],
        jnp.where(col_ids == 1, second_row_dense[:, None], schur),
    )
    return jnp.where(col_ids < row_ids, chosen, 0.0)


def solution(mesh):
    in_specs = (P("row", None, None), P("row", "col", None, None), P("row", "col", None, None), P())
    out_specs = P("row", "col", None, None)
    return jax.shard_map(shards, mesh=mesh, in_specs=in_specs, out_specs=out_specs, check_vma=False)
```

profile of v0, /device:TPU:64, one launch (start us, length us, event | category | flops | bytes accessed | tf_op | source)
XLA Modules:
  0.0 864.5 jit_solution(8564235674343520192)
XLA Ops:
  6.5 1.1 copy.12
  7.8 11.7 %cholesky.130 = f32[128,128]{1,0:T(8,128)S(1)} custom-call(f32[128,128]{1,0:T(8,128)S(1)} %cholesky.194), custom_call_target="Cholesky" | custom-call | tf_op jit(solution)/shard_map/jit(cholesky)/cholesky | solution.py:46
  19.5 9.8 %custom-call.14 = f32[1,128,128]{1,2,0:T(8,128)S(1)} custom-call(f32[1,128,128]{2,1,0:T(8,128)S(1)} %get-tuple-element.96), custom_call_target="InvertDiagBlocksLowerTriangular" | custom-call | tf_op jit(solution)/shard_map/jit(cholesky)/cholesky | solution.py:46
  29.8 11.7 %cholesky.147 = f32[128,128]{1,0:T(8,128)S(1)} custom-call(f32[128,128]{1,0:T(8,128)S(1)} %convolution_subtract_fusion.5), custom_call_target="Cholesky" | custom-call | tf_op jit(solution)/shard_map/jit(cholesky)/cholesky | solution.py:46
  41.6 0.7 compare_reduce_fusion.2
  43.6 0.7 fusion.28
  44.6 0.6 copy-done.10
  45.3 0.7 fusion.51
  46.0 0.6 gather_fusion
  46.9 0.7 select_bitcast_fusion.1
  47.6 155.9 %all-reduce.11.cloned.1.call-done = f32[256,256]{1,0:T(8,128)} async-done(((f32[256,256]{1,0:T(8,128)}), f32[256,256]{1,0:T(8,128)}) %all-reduce.11.cloned.1.call-update) | async-done | bytes 262160 | tf_op jit(solution)/shard_map/psum | solution.py:11
  203.5 1.0 fusion.27
  204.6 4.1 while.7
  204.6 0.6 fusion.102
  205.2 1.4 bitcast_dynamic-update-slice_fusion.4
  206.7 0.6 fusion.102
  207.3 1.4 bitcast_dynamic-update-slice_fusion.4
  208.7 19.7 %custom-call.15 = f32[2,128,128]{1,2,0:T(8,128)S(1)} custom-call(f32[2,128,128]{2,1,0:T(8,128)S(1)} %get-tuple-element.38), custom_call_target="InvertDiagBlocksLowerTriangular" | custom-call | tf_op jit(solution)/shard_map/triangular_solve/custom-call.0 | solution.py:17
  228.9 0.3 fusion.38
  229.2 0.7 maximum_select_fusion
  229.9 109.7 %all-reduce.19.cloned.1.call-done = (f32[256,128]{1,0:T(8,128)}, f32[256,128]{1,0:T(8,128)}) async-done(((f32[256,128]{1,0:T(8,128)}, f32[256,128]{1,0:T(8,128)}), (f32[256,128]{1,0:T(8,128)}, f32[256,128]{1,0:T(8,128)})) %all-reduce.19.cloned.1.call-update) | async-done | bytes 262160 | tf_op jit(solution)/shard_map/psum | solution.py:11
  339.6 1.4 fusion.60
  341.1 0.8 broadcast_select_fusion.8
  342.0 0.8 broadcast_select_fusion.7
  343.1 0.4 convolution_subtract_fusion
  343.7 11.7 %cholesky.164 = f32[128,128]{1,0:T(8,128)S(1)} custom-call(f32[128,128]{1,0:T(8,128)S(1)} %cholesky.197), custom_call_target="Cholesky" | custom-call | tf_op jit(solution)/shard_map/jit(cholesky)/cholesky | solution.py:70
  355.4 9.8 %custom-call.16 = f32[1,128,128]{1,2,0:T(8,128)S(1)} custom-call(f32[1,128,128]{2,1,0:T(8,128)S(1)} %get-tuple-element.92), custom_call_target="InvertDiagBlocksLowerTriangular" | custom-call | tf_op jit(solution)/shard_map/jit(cholesky)/cholesky | solution.py:70
  365.7 11.7 %cholesky.181 = f32[128,128]{1,0:T(8,128)S(1)} custom-call(f32[128,128]{1,0:T(8,128)S(1)} %convolution_subtract_fusion.3), custom_call_target="Cholesky" | custom-call | tf_op jit(solution)/shard_map/jit(cholesky)/cholesky | solution.py:70
  377.5 0.7 compare_reduce_fusion
  378.2 0.6 compare_reduce_fusion.1
  380.2 0.7 select_select_fusion
  381.2 161.0 %all-reduce.15.cloned.1.call-done = (f32[256,128]{1,0:T(8,128)}, f32[256,128]{1,0:T(8,128)}, f32[256,256]{1,0:T(8,128)}) async-done(((f32[256,128]{1,0:T(8,128)}, f32[256,128]{1,0:T(8,128)}, f32[256,256]{1,0:T(8,128)}), (f32[256,128]{1,0:T(8,128)}, f32[256,128]{1,0:T(8,128)}, f32[256,256]{1,0:T(8,128)})) %all-reduce.15.cloned.1.call-update) | async-done | bytes 524304 | tf_op jit(solution)/shard_map/psum | solution.py:11
  542.2 1.0 fusion.25
  543.2 4.1 while.8
  543.2 0.6 fusion.103
  543.8 1.4 bitcast_dynamic-update-slice_fusion.5
  545.2 0.6 fusion.103
  545.8 1.4 bitcast_dynamic-update-slice_fusion.5
  547.3 19.7 %custom-call.17 = f32[2,128,128]{1,2,0:T(8,128)S(1)} custom-call(f32[2,128,128]{2,1,0:T(8,128)S(1)} %get-tuple-element.39), custom_call_target="InvertDiagBlocksLowerTriangular" | custom-call | tf_op jit(solution)/shard_map/triangular_solve/custom-call.0 | solution.py:17
  567.8 0.3 fusion.45
  568.1 0.6 copy-done.8
  568.7 0.4 fusion.63
  569.6 0.7 maximum_select_fusion.1
  570.2 0.9 fusion.8
  571.2 110.5 %all-reduce.17.cloned.1.call-done = (f32[256,128]{1,0:T(8,128)}, f32[256,128]{1,0:T(8,128)}, f32[256,128]{1,0:T(8,128)}) async-done(((f32[256,128]{1,0:T(8,128)}, f32[256,128]{1,0:T(8,128)}, f32[256,128]{1,0:T(8,128)}), (f32[256,128]{1,0:T(8,128)}, f32[256,128]{1,0:T(8,128)}, f32[256,128]{1,0:T(8,128)})) %all-reduce.17.cloned.1.call-update) | async-done | bytes 393232 | tf_op jit(solution)/shard_map/psum | solution.py:11
  681.8 1.7 broadcast_select_fusion.3
  683.4 0.7 broadcast_select_fusion.4
  684.4 0.7 broadcast_select_fusion.5
  685.2 0.4 fusion.59
  685.6 0.4 fusion.62
  686.0 0.5 copy-done.5
  686.5 0.4 convolution_add_fusion.3
  686.9 163.7 %all-reduce.13.cloned.1.call-done = (f32[256,128]{1,0:T(8,128)}, f32[1,256,128]{2,1,0:T(8,128)}, f32[256,128]{1,0:T(8,128)}, f32[256,128]{1,0:T(8,128)}, f32[256...) async-done(((f32[256,128]{1,0:T(8,128)}, f32[1,256,128]{2,1,0:T(8,128)}, f32[256,128]{1,0:T(8,128)}, f32[256,128]{1,0:T(8,128)}, ...) | async-done | bytes 1048592 | tf_op jit(solution)/shard_map/psum | solution.py:11
  850.6 1.4 fusion.64
  852.0 0.4 fusion.6
  852.4 0.5 copy-done.12
  852.9 0.4 fusion.65
  853.3 0.5 copy-done.9
  853.9 0.4 fusion.5
  854.3 0.5 copy-done.15
  854.8 0.6 fusion.12
  855.4 0.6 fusion.21
  856.1 0.6 fusion
  856.7 1.2 fusion.4
  (75 shorter events, 5.1 us)
Async XLA Ops:
  6.5 197.0 %all-reduce.11.cloned.1.call-start = ((), (), s32[]{:S(2)}) async-start(), calls=%async_computation | async-start | bytes 524288 | tf_op jit(solution)/shard_map/psum | solution.py:11
  6.5 1.2 copy-start.3
  44.3 0.9 copy-start.10
  44.3 295.3 %all-reduce.19.cloned.1.call-start = ((), (), s32[]{:S(2)}) async-start(), calls=%async_computation.4 | async-start | bytes 524288 | tf_op jit(solution)/shard_map/psum | solution.py:11
  46.0 0.9 copy-start.4
  229.9 312.3 %all-reduce.15.cloned.1.call-start = ((), (), s32[]{:S(2)}) async-start(), calls=%async_computation.2 | async-start | bytes 1048576 | tf_op jit(solution)/shard_map/psum | solution.py:11
  339.6 1.4 copy-start
  341.1 1.0 copy-start.1
  380.9 300.9 %all-reduce.17.cloned.1.call-start = ((), (), s32[]{:S(2)}) async-start(), calls=%async_computation.3 | async-start | bytes 786432 | tf_op jit(solution)/shard_map/psum | solution.py:11
  547.3 20.0 %copy-start.2 = (f32[256,128]{1,0:T(8,128)S(1)}, f32[256,128]{1,0:T(8,128)}, u32[]{:S(2)}) copy-start(f32[256,128]{1,0:T(8,128)} %get-tuple-element.65) | copy-start | bytes 393220
  567.8 0.9 copy-start.8
  571.2 279.4 %all-reduce.13.cloned.1.call-start = ((), (), s32[]{:S(2)}) async-start(), calls=%async_computation.1 | async-start | bytes 2097152 | tf_op jit(solution)/shard_map/psum | solution.py:11
  681.8 1.7 copy-start.7
  683.4 1.0 copy-start.6
  685.6 0.9 copy-start.5
  850.6 1.4 copy-start.14
  852.0 0.9 copy-start.12
  852.0 1.0 copy-start.13
  852.9 0.9 copy-start.9
  852.9 1.0 copy-start.11
  853.9 0.9 copy-start.15
Sparse Core Ops, SparseCore 0:
  44.5 159.0 all-reduce.10
  230.0 109.6 all-reduce.18
  381.0 161.0 all-reduce.14
  571.3 110.4 all-reduce.16
  686.6 163.9 all-reduce.12
where the time goes:
time: 865 us; the launch traced here: 864 us
  waiting for transfers between devices  701 us (81%)
  other arithmetic  119 us (14%)
  between operations  16.3 us (2%)
  local copies, waits for them, and re-layouts  14.2 us (2%)
  matrix products  13.4 us (2%)
    psum x5, waiting for transfers between devices, from_root(): return lax.psum(jnp.where(mine, shard, jnp.zeros_like(shard)), axis)  701 us
    another operation x5, other arithmetic, lower_solve(): lax.linalg.triangular_solve(factor, flattened, left_side=True, lower=True)  41.3 us
    another operation x7, other arithmetic, shards(): second_pivot = from_root(jnp.linalg.cholesky(shifted), 'row', 1)  34.7 us
    another operation x6, other arithmetic, shards(): first_pivot = from_root(jnp.linalg.cholesky(diag_tiles[0]), 'row', 0)  34 us
  transfers between devices with their start and end apart: 5, of which 5 were waited for; matrix products, arithmetic and copies ran while one was open for 0% of the time, Pallas kernels for 0%

commit v1 on v0

--- a/solution.py
+++ b/solution.py
@@ -8,7 +8,7 @@
 
 def from_root(shard, axis, root):
     mine = lax.axis_index(axis) == root
-    return lax.psum(jnp.where(mine, shard, jnp.zeros_like(shard)), axis)
+    return jnp.sum(lax.all_gather(jnp.where(mine, shard, jnp.zeros_like(shard)), axis), axis=0)
 
 
 def lower_solve(factor, stacked):

time: 865 us -> 1410 us (1.63)
  the two profiles are of different devices: /device:TPU:64 before, /device:TPU:8 now
where the time goes in v1:
time: 1410 us; the launch traced here: 1400 us
  waiting for transfers between devices  1200 us (85%)
  other arithmetic  158 us (11%)
  between operations  16.7 us (1%)
    all_gather x17, waiting for transfers between devices, from_root(): lax.all_gather(jnp.where(mine, shard, jnp.zeros_like(shard)), axis)  1200 us
    another operation x5, other arithmetic, lower_solve(): lax.linalg.triangular_solve(factor, flattened, left_side=True, lower=True)  39.4 us
    reduce_sum x16, other arithmetic, from_root(): jnp.sum(lax.all_gather(jnp.where(mine, shard, jnp.zeros_like(shard)), axi...  38.6 us
    another operation x7, other arithmetic, shards(): second_pivot = from_root(jnp.linalg.cholesky(shifted), 'row', 1)  34.7 us
    another operation x6, other arithmetic, shards(): first_pivot = from_root(jnp.linalg.cholesky(diag_tiles[0]), 'row', 0)  34 us
  transfers between devices with their start and end apart: 17, of which 17 were waited for; matrix products, arithmetic and copies ran while one was open for 7% of the time, Pallas kernels for 0%

profile of v1, /device:TPU:8, one launch (start us, length us, event | category | flops | bytes accessed | tf_op | source)
XLA Modules:
  0.0 1401.2 jit_solution(2309819090814478668)
XLA Ops:
  6.5 1.1 copy.17
  7.7 1.0 fusion.19
  8.7 11.7 cholesky.130
  20.4 9.8 custom-call.14
  30.7 11.7 cholesky.147
  42.5 0.7 compare_reduce_fusion.2
  44.6 0.7 fusion.28
  45.4 0.7 fusion.51
  46.8 0.9 convert_select_fusion
  47.8 0.7 slice_select_fusion
  49.1 103.1 %all-gather.37.cloned.1.call-done = f32[8192,256]{1,0:T(8,128)} async-done(((f32[256,256]{1,0:T(8,128)}), f32[8192,256]{1,0:T(8,128)}) %all-gather.37.cloned.1.call-update) | async-done | bytes 8388624 | tf_op jit(solution)/shard_map/all_gather | solution.py:11
  152.1 3.9 reduce_sum.154
  156.2 4.0 while.7
  156.8 1.4 bitcast_dynamic-update-slice_fusion.4
  158.8 1.4 bitcast_dynamic-update-slice_fusion.4
  160.1 19.7 %custom-call.15 = f32[2,128,128]{1,2,0:T(8,128)S(1)} custom-call(f32[2,128,128]{2,1,0:T(8,128)S(1)} %get-tuple-element.38), custom_call_target="InvertDiagBlocksLowerTriangular" | custom-call | tf_op jit(solution)/shard_map/triangular_solve/custom-call.0 | solution.py:17
  181.4 15.2 %all-gather.33.cloned.1.call-done = f32[16,1,256,128]{3,2,1,0:T(8,128)} async-done(((f32[1,1,256,128]{3,2,1,0:T(8,128)}), f32[16,1,256,128]{3,2,1,0:T(8,128)}) %all-gather.33.cloned.1.call-update) | async-done | bytes 2097168 | tf_op jit(solution)/shard_map/all_gather | solution.py:11
  196.5 1.7 reduce_sum.153
  198.2 41.5 %all-gather.39.cloned.1.call-done = f32[4096,128]{1,0:T(8,128)} async-done(((f32[256,128]{1,0:T(8,128)}), f32[4096,128]{1,0:T(8,128)}) %all-gather.39.cloned.1.call-update) | async-done | bytes 2097168 | tf_op jit(solution)/shard_map/all_gather | solution.py:11
  239.8 1.7 reduce.13
  242.7 11.7 cholesky.164
  254.5 9.8 custom-call.16
  264.8 11.7 cholesky.181
  276.5 0.7 compare_reduce_fusion
  279.2 0.7 select_select_fusion
  280.1 0.7 broadcast_select_fusion.8
  280.8 0.7 broadcast_select_fusion.9
  282.5 97.8 %all-gather.41.cloned.1.call-done = f32[8192,256]{1,0:T(8,128)} async-done(((f32[256,256]{1,0:T(8,128)}), f32[8192,256]{1,0:T(8,128)}) %all-gather.41.cloned.1.call-update) | async-done | bytes 8388624 | tf_op jit(solution)/shard_map/all_gather | solution.py:11
  380.3 3.9 reduce_sum.157
  384.3 4.1 while.8
  384.9 1.4 bitcast_dynamic-update-slice_fusion.5
  387.0 1.4 bitcast_dynamic-update-slice_fusion.5
  388.4 19.7 %custom-call.17 = f32[2,128,128]{1,2,0:T(8,128)S(1)} custom-call(f32[2,128,128]{2,1,0:T(8,128)S(1)} %get-tuple-element.39), custom_call_target="InvertDiagBlocksLowerTriangular" | custom-call | tf_op jit(solution)/shard_map/triangular_solve/custom-call.0 | solution.py:17
  409.6 60.1 %all-gather.47.cloned.1.call-done = f32[8192,128]{1,0:T(8,128)} async-done(((f32[256,128]{1,0:T(8,128)}), f32[8192,128]{1,0:T(8,128)}) %all-gather.47.cloned.1.call-update) | async-done | bytes 4194320 | tf_op jit(solution)/shard_map/all_gather | solution.py:11
  469.8 2.4 reduce_sum.160
  472.2 85.3 %all-gather.45.cloned.1.call-done = f32[8192,128]{1,0:T(8,128)} async-done(((f32[256,128]{1,0:T(8,128)}), f32[8192,128]{1,0:T(8,128)}) %all-gather.45.cloned.1.call-update) | async-done | bytes 4194320 | tf_op jit(solution)/shard_map/all_gather | solution.py:11
  557.4 2.4 reduce_sum.159
  561.3 0.8 copy.21
  562.1 38.0 %all-gather.35.cloned.1.call-done = f32[16,1,256,128]{3,2,1,0:T(8,128)} async-done(((f32[1,1,256,128]{3,2,1,0:T(8,128)}), f32[16,1,256,128]{3,2,1,0:T(8,128)}) %all-gather.35.cloned.1.call-update) | async-done | bytes 2097168 | tf_op jit(solution)/shard_map/all_gather | solution.py:11
  600.1 1.7 reduce_sum.156
  601.8 0.7 broadcast_select_fusion.5
  604.6 38.9 %all-gather.43.cloned.1.call-done = f32[4096,128]{1,0:T(8,128)} async-done(((f32[256,128]{1,0:T(8,128)}), f32[4096,128]{1,0:T(8,128)}) %all-gather.43.cloned.1.call-update) | async-done | bytes 2097168 | tf_op jit(solution)/shard_map/all_gather | solution.py:11
  643.5 1.7 reduce.14
  645.2 0.7 broadcast_select_fusion.4
  646.0 40.9 %all-gather.49.cloned.1.call-done = f32[16,256,128]{2,1,0:T(8,128)} async-done(((f32[1,256,128]{2,1,0:T(8,128)}), f32[16,256,128]{2,1,0:T(8,128)}) %all-gather.49.cloned.1.call-update) | async-done | bytes 2097168 | tf_op jit(solution)/shard_map/all_gather | solution.py:11
  686.9 1.7 reduce.15
  688.6 0.7 broadcast_select_fusion.3
  690.6 84.8 %all-gather.55.cloned.1.call-done = f32[8192,128]{1,0:T(8,128)} async-done(((f32[256,128]{1,0:T(8,128)}), f32[8192,128]{1,0:T(8,128)}) %all-gather.55.cloned.1.call-update) | async-done | bytes 4194320 | tf_op jit(solution)/shard_map/all_gather | solution.py:11
  775.4 2.4 reduce_sum.164
  777.8 85.4 %all-gather.61.cloned.1.call-done = f32[8192,128]{1,0:T(8,128)} async-done(((f32[256,128]{1,0:T(8,128)}), f32[8192,128]{1,0:T(8,128)}) %all-gather.61.cloned.1.call-update) | async-done | bytes 4194320 | tf_op jit(solution)/shard_map/all_gather | solution.py:11
  863.2 2.4 reduce_sum.167
  865.6 85.3 %all-gather.51.cloned.1.call-done = f32[8192,128]{1,0:T(8,128)} async-done(((f32[256,128]{1,0:T(8,128)}), f32[8192,128]{1,0:T(8,128)}) %all-gather.51.cloned.1.call-update) | async-done | bytes 4194320 | tf_op jit(solution)/shard_map/all_gather | solution.py:11
  950.9 2.4 reduce_sum.162
  953.7 85.0 %all-gather.53.cloned.1.call-done = f32[8192,128]{1,0:T(8,128)} async-done(((f32[256,128]{1,0:T(8,128)}), f32[8192,128]{1,0:T(8,128)}) %all-gather.53.cloned.1.call-update) | async-done | bytes 4194320 | tf_op jit(solution)/shard_map/all_gather | solution.py:11
  1038.7 2.4 reduce_sum.163
  1043.1 83.3 %all-gather.57.cloned.1.call-done = f32[8192,128]{1,0:T(8,128)} async-done(((f32[256,128]{1,0:T(8,128)}), f32[8192,128]{1,0:T(8,128)}) %all-gather.57.cloned.1.call-update) | async-done | bytes 4194320 | tf_op jit(solution)/shard_map/all_gather | solution.py:11
  1126.3 2.4 reduce_sum.165
  1128.7 85.3 %all-gather.59.cloned.1.call-done = f32[8192,128]{1,0:T(8,128)} async-done(((f32[256,128]{1,0:T(8,128)}), f32[8192,128]{1,0:T(8,128)}) %all-gather.59.cloned.1.call-update) | async-done | bytes 4194320 | tf_op jit(solution)/shard_map/all_gather | solution.py:11
  1214.0 2.4 reduce_sum.166
  1216.4 85.3 %all-gather.65.cloned.1.call-done = f32[8192,128]{1,0:T(8,128)} async-done(((f32[256,128]{1,0:T(8,128)}), f32[8192,128]{1,0:T(8,128)}) %all-gather.65.cloned.1.call-update) | async-done | bytes 4194320 | tf_op jit(solution)/shard_map/all_gather | solution.py:11
  1301.7 2.4 reduce_sum.169
  1304.9 84.5 %all-gather.63.cloned.1.call-done = f32[8192,128]{1,0:T(8,128)} async-done(((f32[256,128]{1,0:T(8,128)}), f32[8192,128]{1,0:T(8,128)}) %all-gather.63.cloned.1.call-update) | async-done | bytes 4194320 | tf_op jit(solution)/shard_map/all_gather | solution.py:11
  1389.4 2.4 reduce_sum.168
  1393.2 1.2 fusion.4
  (101 shorter events, 20.2 us)
Async XLA Ops:
  6.5 42.5 %copy-start.1 = (bf16[1,2,256,128]{3,2,1,0:T(8,128)(2,1)S(1)}, bf16[1,2,256,128]{3,2,1,0:T(8,128)(2,1)}, u32[]{:S(2)}) copy-start(bf16[1,2,256,128]{3,2,1,0:T(8,128)(2,1)} %param.9) | copy-start | bytes 393220
  6.5 145.6 %all-gather.37.cloned.1.call-start = ((), (), s32[]{:S(2)}) async-start(), calls=%async_computation.2 | async-start | bytes 8650752 | tf_op jit(solution)/shard_map/all_gather | solution.py:11
  45.3 151.2 %all-gather.33.cloned.1.call-start = ((), (), s32[]{:S(2)}) async-start(), calls=%async_computation | async-start | bytes 2228224 | tf_op jit(solution)/shard_map/all_gather | solution.py:11
  48.5 191.2 %all-gather.39.cloned.1.call-start = ((), (), s32[]{:S(2)}) async-start(), calls=%async_computation.3 | async-start | bytes 2228224 | tf_op jit(solution)/shard_map/all_gather | solution.py:11
  181.3 199.0 %all-gather.41.cloned.1.call-start = ((), (), s32[]{:S(2)}) async-start(), calls=%async_computation.4 | async-start | bytes 8650752 | tf_op jit(solution)/shard_map/all_gather | solution.py:11
  280.0 189.8 %all-gather.47.cloned.1.call-start = ((), (), s32[]{:S(2)}) async-start(), calls=%async_computation.7 | async-start | bytes 4325376 | tf_op jit(solution)/shard_map/all_gather | solution.py:11
  280.8 276.6 %all-gather.45.cloned.1.call-start = ((), (), s32[]{:S(2)}) async-start(), calls=%async_computation.6 | async-start | bytes 4325376 | tf_op jit(solution)/shard_map/all_gather | solution.py:11
  281.6 318.5 %all-gather.35.cloned.1.call-start = ((), (), s32[]{:S(2)}) async-start(), calls=%async_computation.1 | async-start | bytes 2228224 | tf_op jit(solution)/shard_map/all_gather | solution.py:11
  282.3 361.2 %all-gather.43.cloned.1.call-start = ((), (), s32[]{:S(2)}) async-start(), calls=%async_computation.5 | async-start | bytes 2228224 | tf_op jit(solution)/shard_map/all_gather | solution.py:11
  409.6 277.4 %all-gather.49.cloned.1.call-start = ((), (), s32[]{:S(2)}) async-start(), calls=%async_computation.8 | async-start | bytes 2228224 | tf_op jit(solution)/shard_map/all_gather | solution.py:11
  562.1 213.3 %all-gather.55.cloned.1.call-start = ((), (), s32[]{:S(2)}) async-start(), calls=%async_computation.11 | async-start | bytes 4325376 | tf_op jit(solution)/shard_map/all_gather | solution.py:11
  602.5 260.7 %all-gather.61.cloned.1.call-start = ((), (), s32[]{:S(2)}) async-start(), calls=%async_computation.14 | async-start | bytes 4325376 | tf_op jit(solution)/shard_map/all_gather | solution.py:11
  603.2 347.6 %all-gather.51.cloned.1.call-start = ((), (), s32[]{:S(2)}) async-start(), calls=%async_computation.9 | async-start | bytes 4325376 | tf_op jit(solution)/shard_map/all_gather | solution.py:11
  603.8 434.9 %all-gather.53.cloned.1.call-start = ((), (), s32[]{:S(2)}) async-start(), calls=%async_computation.10 | async-start | bytes 4325376 | tf_op jit(solution)/shard_map/all_gather | solution.py:11
  604.6 521.8 %all-gather.57.cloned.1.call-start = ((), (), s32[]{:S(2)}) async-start(), calls=%async_computation.12 | async-start | bytes 4325376 | tf_op jit(solution)/shard_map/all_gather | solution.py:11
  645.9 568.1 %all-gather.59.cloned.1.call-start = ((), (), s32[]{:S(2)}) async-start(), calls=%async_computation.13 | async-start | bytes 4325376 | tf_op jit(solution)/shard_map/all_gather | solution.py:11
  689.4 612.3 %all-gather.65.cloned.1.call-start = ((), (), s32[]{:S(2)}) async-start(), calls=%async_computation.16 | async-start | bytes 4325376 | tf_op jit(solution)/shard_map/all_gather | solution.py:11
  690.0 699.4 %all-gather.63.cloned.1.call-start = ((), (), s32[]{:S(2)}) async-start(), calls=%async_computation.15 | async-start | bytes 4325376 | tf_op jit(solution)/shard_map/all_gather | solution.py:11
  1304.5 88.7 %copy-start = (bf16[1,2,256,128]{3,2,1,0:T(8,128)(2,1)S(1)}, bf16[1,2,256,128]{3,2,1,0:T(8,128)(2,1)}, u32[]{:S(2)}) copy-start(bf16[1,2,256,128]{3,2,1,0:T(8,128)(2,1)} %param.8) | copy-start | bytes 393220
Sparse Core Ops, SparseCore 0:
  45.4 106.6 all-gather.36
  154.2 42.2 all-gather.32
  198.7 41.0 all-gather.38
  280.1 100.1 all-gather.40
  383.3 86.3 all-gather.46
  472.8 84.6 all-gather.44
  559.5 40.4 all-gather.34
  602.2 41.2 all-gather.42
  645.6 41.2 all-gather.48
  689.9 85.3 all-gather.54
  778.6 84.6 all-gather.60
  866.2 84.6 all-gather.50
  954.0 84.5 all-gather.52
  1041.7 84.5 all-gather.56
  1129.4 84.6 all-gather.58
  1217.0 84.6 all-gather.64
  1304.7 84.6 all-gather.62
